TPU v7x, 32 devices: a whole 2x2x4 slice. The times are simulated.
32 devices in a mesh: ctx: 16 (over z, y, core), kvh: 2 (over x).
Axes of the slice: x: 2, y: 2, z: 4, core: 2. Of those that a mesh axis runs over, the one named last changes fastest.
Arguments:
- queries: bfloat16 [4096, 64, 128], P('ctx', 'kvh'), may hold values from -110 to 110
- key_value: bfloat16 [2, 4096, 8, 128], P(None, 'ctx', 'kvh'), may hold values from -5 to 5
- span_table: int32 [32], replicated, may hold values from 0 to 31, as said below
Outputs:
- attended: bfloat16 [4096, 8192], P(('ctx', 'kvh'))
Inputs may be any that keep to these rules, and one draw needn't show every extreme that they name: `span_table`: entries 2 d and 2 d + 1 are the spans of ctx index d: the first below 16, the second 16 or above; every span of 0 to 31 appears exactly once.
All inputs are finite; a program needn't handle non-finite values.
Results may differ from a plain program's by a relative error of at most 0.0065.
Values may be sent and summed in bfloat16 or wider, within the bound.
A program may use at most 64 MiB of HBM per device.

v0:
```python
import jax
import jax.numpy as jnp
from jax import lax
from jax.sharding import PartitionSpec as P

STEPS = 4


def passed_along(value, axis, steps):
    count = lax.axis_size(axis)
    pairs = [(source, (source + steps) % count) for source in range(count)]
    return lax.ppermute(value, axis, pairs)


def body(queries, key_value, span_table):
    rows = queries.shape[0]
    heads_here = queries.shape[1]
    head_size = queries.shape[2]
    kv_here = key_value.shape[2]
    group = heads_here // kv_here
    span = rows // 2
    scale = 1.0 / head_size**0.5
    cycle = lax.axis_size("ctx")
    myself = lax.axis_index("ctx")
    table = span_table.reshape(cycle, 2)
    offsets = jnp.arange(span, dtype=jnp.int32)

    def positions_of(device):
        pair = lax.dynamic_index_in_dim(table, device, 0, keepdims=False)
        return (pair[:, None] * span + offsets[None, :]).reshape(rows)

    query_pos = positions_of(myself)
    grouped = queries.reshape(rows, kv_here, group, head_size)

    def attend(carry, block, source):
        run_max, numer, denom = carry
        key_pos = positions_of(source)
        scores = (
            jnp.einsum("qghd,kgd->ghqk", grouped, block[0], preferred_element_type=jnp.float32)
            * scale
        )
        visible = (key_pos[None, :] <= query_pos[:, None])[None, None]
        masked = jnp.where(visible, scores, -jnp.inf)
        block_max = jnp.maximum(jnp.max(masked, axis=-1), jnp.float32(-1e30))
        weight = jnp.exp(masked - block_max[..., None])
        block_sum = jnp.sum(weight, axis=-1)
        block_out = jnp.einsum(
            "ghqk,kgd->ghqd",
            weight.astype(jnp.bfloat16),
            block[1],
            preferred_element_type=jnp.float32,
        )
        new_max = jnp.maximum(run_max, block_max)
        old_factor = jnp.exp(run_max - new_max)
        new_factor = jnp.exp(block_max - new_max)
        numer = numer * old_factor[..., None] + block_out * new_factor[..., None]
        denom = denom * old_factor + block_sum * new_factor
        return (new_max, numer, denom)

    start = (
        jnp.full((kv_here, group, rows), -1e30, jnp.float32),
        jnp.zeros((kv_here, group, rows, head_size), jnp.float32),
        jnp.zeros((kv_here, group, rows), jnp.float32),
    )
    carry = attend(start, key_value, myself)
    moving = key_value
    for distance in range(1, STEPS):
        moving = passed_along(moving, "ctx", 1)
        carry = attend(carry, moving, (myself - distance) % cycle)
    run_max, numer, denom = carry
    result = numer / denom[..., None]
    local_out = (
        jnp.transpose(result, (2, 0, 1, 3))
        .reshape(rows, heads_here * head_size)
        .astype(jnp.bfloat16)
    )
    return lax.all_to_all(local_out, "kvh", split_axis=0, concat_axis=1, tiled=True)


def solution(mesh):
    in_specs = (P("ctx", "kvh", None), P(None, "ctx", "kvh", None), P())
    out_specs = P(("ctx", "kvh"), None)
    return jax.shard_map(body, mesh=mesh, in_specs=in_specs, out_specs=out_specs, check_vma=False)
```

profile of v0, /device:TPU:0, one launch (start us, length us, event | category | flops | bytes accessed | tf_op | source)
XLA Modules:
  0.0 94.8 jit_solution(17299395161317736127)
XLA Ops:
  0.0 0.0 copy-start
  0.0 1.3 %copy.27 = bf16[2,256,4,128]{3,1,2,0:T(8,128)(2,1)S(1)} copy(bf16[2,256,4,128]{3,2,1,0:T(4,128)(2,1)} %param.4) | data formatting | bytes 1048576 | tf_op args[1]
  1.3 0.5 collective-permute-start
  1.8 0.7 reshape.328
  2.5 0.1 add_bitcast_fusion
  2.6 0.1 add_bitcast_fusion.2
  2.7 0.2 broadcast_compare_fusion
  2.9 0.0 copy-done
  2.9 2.1 %fusion.8 = (f32[4,8,256]{2,1,0:T(8,128)S(1)}, f32[4,256,256,8]{2,1,3,0:T(8,128)S(1)}) fusion(pred[256,256]{0,1:T(8,128)(4,1)S(1)} %get-tuple-element.23, bf16[256,4,8,128]{3,2,1,0:T(8,128)(2,1)S(1)} %bitcast.239, bf16[2,256,4,128]{3,1,2,0:T(8,128)(2,1)S(1)} %copy.27), kind=kOutput, calls=%fused_computation.16 | convolution fusion | flops 543154176 | bytes 10846208 | tf_op jit(solution)/shard_map/qghd,kgd->ghqk/dot_general | solution.py:39
  5.0 2.4 %fusion.18 = f32[4,8,256,128]{3,2,1,0:T(8,128)S(1)} fusion(f32[4,256,256,8]{2,1,3,0:T(8,128)S(1)} %get-tuple-element.30, f32[4,8,256]{2,1,0:T(8,128)S(1)} %broadcast_maximum_fusion.3, pred[256,256]{0,1:T(8,128)(4,1)S(1)} %get-tuple-element.23, bf16[2,256,4,128]{3,1,2,0:T(8,128)(2,1)S(1)} %copy.27), kind=kOutput, calls=%fused_computation.23 | convolution fusion | flops 545259520 | bytes 12943360 | tf_op jit(solution)/shard_map/ghqk,kgd->ghqd/dot_general | solution.py:47
  7.4 1.8 %fusion = f32[4,8,256]{2,1,0:T(8,128)S(1)} fusion(f32[4,256,256,8]{2,1,3,0:T(8,128)S(1)} %get-tuple-element.30, f32[4,8,256]{2,1,0:T(8,128)S(1)} %broadcast_maximum_fusion.3, pred[256,256]{0,1:T(8,128)(4,1)S(1)} %get-tuple-element.23), kind=kLoop, calls=%fused_computation.8 | loop fusion | flops 8380416 | bytes 8519680 | tf_op jit(solution)/shard_map/reduce_sum | solution.py:46
  9.2 4.4 %collective-permute-done = bf16[2,256,4,128]{3,1,2,0:T(8,128)(2,1)S(1)} collective-permute-done((bf16[2,256,4,128]{3,1,2,0:T(8,128)(2,1)S(1)}, bf16[2,256,4,128]{3,1,2,0:T(8,128)(2,1)S(1)}, u32[]{:S(2)}, u32[]{:S(2)}) %collective-permute-start) | collective-permute-done | bytes 524320 | tf_op jit(solution)/shard_map/ppermute | solution.py:12
  13.6 2.1 %fusion.9 = (f32[4,8,256]{2,1,0:T(8,128)S(1)}, f32[4,256,256,8]{2,1,3,0:T(8,128)S(1)}) fusion(pred[256,256]{0,1:T(8,128)(4,1)S(1)} %get-tuple-element.24, bf16[256,4,8,128]{3,2,1,0:T(8,128)(2,1)S(1)} %bitcast.242, bf16[2,256,4,128]{3,1,2,0:T(8,128)(2,1)S(1)} %collective-permute-done), kind=kOutput, calls=%fused_computation.17 | convolution fusion | flops 543154176 | bytes 10846208 | tf_op jit(solution)/shard_map/qghd,kgd->ghqk/dot_general | solution.py:39
  15.8 0.2 collective-permute-start.1
  16.0 2.4 %fusion.16 = f32[4,8,256,128]{3,2,1,0:T(8,128)S(1)} fusion(f32[4,256,256,8]{2,1,3,0:T(8,128)S(1)} %get-tuple-element.28, f32[4,8,256]{2,1,0:T(8,128)S(1)} %broadcast_maximum_fusion.2, pred[256,256]{0,1:T(8,128)(4,1)S(1)} %get-tuple-element.24, bf16[2,256,4,128]{3,1,2,0:T(8,128)(2,1)S(1)} %collective-permute-done), kind=kOutput, calls=%fused_computation.22 | convolution fusion | flops 545259520 | bytes 12943360 | tf_op jit(solution)/shard_map/ghqk,kgd->ghqd/dot_general | solution.py:47
  18.4 1.8 %fusion.2 = f32[4,8,256]{2,1,0:T(8,128)S(1)} fusion(f32[4,256,256,8]{2,1,3,0:T(8,128)S(1)} %get-tuple-element.28, f32[4,8,256]{2,1,0:T(8,128)S(1)} %broadcast_maximum_fusion.2, pred[256,256]{0,1:T(8,128)(4,1)S(1)} %get-tuple-element.24), kind=kLoop, calls=%fused_computation.10 | loop fusion | flops 8380416 | bytes 8519680 | tf_op jit(solution)/shard_map/reduce_sum | solution.py:46
  20.2 7.1 %collective-permute-done.1 = bf16[2,256,4,128]{3,1,2,0:T(8,128)(2,1)S(1)} collective-permute-done((bf16[2,256,4,128]{3,1,2,0:T(8,128)(2,1)S(1)}, bf16[2,256,4,128]{3,1,2,0:T(8,128)(2,1)S(1)}, u32[]{:S(2)}, u32[]{:S(2)}) %collective-permute-start.1) | collective-permute-done | bytes 524320 | tf_op jit(solution)/shard_map/ppermute | solution.py:12
  27.3 2.1 %fusion.10 = (f32[4,8,256]{2,1,0:T(8,128)S(1)}, f32[4,256,256,8]{2,1,3,0:T(8,128)S(1)}) fusion(pred[256,256]{0,1:T(8,128)(4,1)S(1)} %get-tuple-element.22, bf16[256,4,8,128]{3,2,1,0:T(8,128)(2,1)S(1)} %bitcast.241, bf16[2,256,4,128]{3,1,2,0:T(8,128)(2,1)S(1)} %collective-permute-done.1), kind=kOutput, calls=%fused_computation.18 | convolution fusion | flops 543154176 | bytes 10846208 | tf_op jit(solution)/shard_map/qghd,kgd->ghqk/dot_general | solution.py:39
  29.5 0.3 collective-permute-start.2
  29.8 2.4 %fusion.14 = f32[4,8,256,128]{3,2,1,0:T(8,128)S(1)} fusion(f32[4,256,256,8]{2,1,3,0:T(8,128)S(1)} %get-tuple-element.26, f32[4,8,256]{2,1,0:T(8,128)S(1)} %broadcast_maximum_fusion.1, pred[256,256]{0,1:T(8,128)(4,1)S(1)} %get-tuple-element.22, bf16[2,256,4,128]{3,1,2,0:T(8,128)(2,1)S(1)} %collective-permute-done.1), kind=kOutput, calls=%fused_computation.21 | convolution fusion | flops 545259520 | bytes 12943360 | tf_op jit(solution)/shard_map/ghqk,kgd->ghqd/dot_general | solution.py:47
  32.2 1.8 %fusion.4 = f32[4,8,256]{2,1,0:T(8,128)S(1)} fusion(f32[4,256,256,8]{2,1,3,0:T(8,128)S(1)} %get-tuple-element.26, f32[4,8,256]{2,1,0:T(8,128)S(1)} %broadcast_maximum_fusion.1, pred[256,256]{0,1:T(8,128)(4,1)S(1)} %get-tuple-element.22), kind=kLoop, calls=%fused_computation.12 | loop fusion | flops 8380416 | bytes 8519680 | tf_op jit(solution)/shard_map/reduce_sum | solution.py:46
  34.0 7.1 %collective-permute-done.2 = bf16[2,256,4,128]{3,1,2,0:T(8,128)(2,1)S(1)} collective-permute-done((bf16[2,256,4,128]{3,1,2,0:T(8,128)(2,1)S(1)}, bf16[2,256,4,128]{3,1,2,0:T(8,128)(2,1)S(1)}, u32[]{:S(2)}, u32[]{:S(2)}) %collective-permute-start.2) | collective-permute-done | bytes 524320 | tf_op jit(solution)/shard_map/ppermute | solution.py:12
  41.1 2.1 %fusion.11 = (f32[4,8,256]{2,1,0:T(8,128)S(1)}, f32[4,256,256,8]{2,1,3,0:T(8,128)S(1)}) fusion(pred[256,256]{0,1:T(8,128)(4,1)S(1)} %get-tuple-element.21, bf16[256,4,8,128]{3,2,1,0:T(8,128)(2,1)S(1)} %bitcast.240, bf16[2,256,4,128]{3,1,2,0:T(8,128)(2,1)S(1)} %collective-permute-done.2), kind=kOutput, calls=%fused_computation.19 | convolution fusion | flops 543154176 | bytes 10846208 | tf_op jit(solution)/shard_map/qghd,kgd->ghqk/dot_general | solution.py:39
  43.2 1.8 %fusion.6 = f32[4,8,256]{2,1,0:T(8,128)S(1)} fusion(f32[4,256,256,8]{2,1,3,0:T(8,128)S(1)} %get-tuple-element.32, f32[4,8,256]{2,1,0:T(8,128)S(1)} %broadcast_maximum_fusion, pred[256,256]{0,1:T(8,128)(4,1)S(1)} %get-tuple-element.21), kind=kLoop, calls=%fused_computation.14 | loop fusion | flops 8380416 | bytes 8519680 | tf_op jit(solution)/shard_map/reduce_sum | solution.py:46
  45.0 0.1 fusion.57
  45.1 12.3 %fusion.22 = bf16[256,4,8,128]{3,0,2,1:T(8,128)(2,1)S(1)} fusion(f32[4,8,256,128]{3,2,1,0:T(8,128)S(1)} %fusion.14, f32[4,8,256,128]{3,2,1,0:T(8,128)S(1)} %fusion.16, f32[4,8,256,128]{3,2,1,0:T(8,128)S(1)} %fusion.18, f32[256,4,8]{0,2,1:T(8,128)S(1)} %get-tuple-element.7, f32[256,4,8]{0,2,1:T(8,128)S(1)} %get-tuple-element.10, ...), kind=kOutput, calls=%fused_computation.27 | convolution fusion | flops 558891008 | bytes 23724032 | tf_op jit(solution)/shard_map/ghqk,kgd->ghqd/dot_general | solution.py:47
  57.4 2.7 %copy.38 = bf16[256,4,8,128]{3,2,1,0:T(8,128)(2,1)} copy(bf16[256,4,8,128]{3,0,2,1:T(8,128)(2,1)S(1)} %fusion.22) | data formatting | bytes 4194304 | tf_op jit(solution)/shard_map/convert_element_type | solution.py:75
  60.0 4.2 %convert_element_type.24 = bf16[2,128,4096]{2,1,0:T(8,128)(2,1)} reshape(bf16[256,4,8,128]{3,2,1,0:T(8,128)(2,1)} %copy.38) | data formatting | bytes 4194304 | tf_op jit(solution)/shard_map/convert_element_type | solution.py:75
  64.2 22.4 %all_to_all.16 = bf16[2,128,4096]{2,1,0:T(8,128)(2,1)} all-to-all(bf16[2,128,4096]{2,1,0:T(8,128)(2,1)} %convert_element_type.24), channel_id=1, replica_groups=mesh['ctx'=16,'kvh'=2] {'kvh'}, dimensions={0} | all-to-all | bytes 4194304 | tf_op jit(solution)/shard_map/all_to_all | solution.py:77
  86.6 4.1 %copy.39 = bf16[128,2,4096]{0,2,1:T(8,128)(2,1)} copy(bf16[128,2,4096]{2,0,1:T(8,128)(2,1)} %bitcast.243) | data formatting | bytes 4194304 | tf_op jit(solution)/shard_map/all_to_all | solution.py:77
  90.7 4.1 %copy.40 = bf16[128,8192]{1,0:T(8,128)(2,1)} copy(bf16[128,8192]{0,1:T(8,128)(2,1)} %bitcast.244) | data formatting | bytes 4194304 | tf_op jit(solution)/shard_map/all_to_all | solution.py:77
  (6 shorter events, 0.1 us)
Async XLA Ops:
  0.0 2.9 %copy-start = (bf16[256,32,128]{2,1,0:T(8,128)(2,1)S(1)}, bf16[256,32,128]{2,1,0:T(8,128)(2,1)}, u32[]{:S(2)}) copy-start(bf16[256,32,128]{2,1,0:T(8,128)(2,1)} %param.3) | copy-start | bytes 6291460
  1.3 12.4 %collective-permute-start = (bf16[2,256,4,128]{3,1,2,0:T(8,128)(2,1)S(1)}, bf16[2,256,4,128]{3,1,2,0:T(8,128)(2,1)S(1)}, u32[]{:S(2)}, u32[]{:S(2)}) collective-permute-start(bf16[2,256,4,128]{3,1,2,0:T(8,128)(2,1)S(1)} %copy.27), channel_id=1, source_target_pairs={{0,2},{2,4},{4,6},{6,8},{8,10},{10,12},{12,14},{14,16},{16,18},{18... | collective-permute-start | bytes 1572872 | tf_op jit(solution)/shard_map/ppermute | solution.py:12
  15.8 11.5 %collective-permute-start.1 = (bf16[2,256,4,128]{3,1,2,0:T(8,128)(2,1)S(1)}, bf16[2,256,4,128]{3,1,2,0:T(8,128)(2,1)S(1)}, u32[]{:S(2)}, u32[]{:S(2)}) collective-permute-start(bf16[2,256,4,128]{3,1,2,0:T(8,128)(2,1)S(1)} %collective-permute-done), channel_id=1, source_target_pairs={{0,2},{2,4},{4,6},{6,8},{8,10},{10,12},{12,14},{14,16},{16,18},{18... | collective-permute-start | bytes 1572872 | tf_op jit(solution)/shard_map/ppermute | solution.py:12
  29.5 11.6 %collective-permute-start.2 = (bf16[2,256,4,128]{3,1,2,0:T(8,128)(2,1)S(1)}, bf16[2,256,4,128]{3,1,2,0:T(8,128)(2,1)S(1)}, u32[]{:S(2)}, u32[]{:S(2)}) collective-permute-start(bf16[2,256,4,128]{3,1,2,0:T(8,128)(2,1)S(1)} %collective-permute-done.1), channel_id=1, source_target_pairs={{0,2},{2,4},{4,6},{6,8},{8,10},{10,12},{12,14},{14,16},{16,18},{18... | collective-permute-start | bytes 1572872 | tf_op jit(solution)/shard_map/ppermute | solution.py:12
where the time goes:
time: 95.9 us; the launch traced here: 94.8 us
  matrix products  27.8 us (29%)
  blocking collectives  22.4 us (23%)
  waiting for transfers between devices  18.7 us (19%)
  local copies, waits for them, and re-layouts  17 us (18%)
  other arithmetic  7.65 us (8%)
  starting transfers between devices  1.02 us (1%)
    all_to_all x1, blocking collectives, body(): lax.all_to_all(local_out, 'kvh', split_axis=0, concat_axis=1, tiled=True)  22.4 us
    dot_general x4, matrix products, attend(): jnp.einsum('ghqk,kgd->ghqd', weight.astype(jnp.bfloat16), block[1], prefe...  19.3 us
    ppermute x3, waiting for transfers between devices, passed_along(): return lax.ppermute(value, axis, pairs)  18.7 us
    dot_general x4, matrix products, attend(): jnp.einsum('qghd,kgd->ghqk', grouped, block[0], preferred_element_type=jn...  8.5 us
    all_to_all x2, local copies, waits for them, and re-layouts, body(): lax.all_to_all(local_out, 'kvh', split_axis=0, concat_axis=1, tiled=True)  8.14 us
    reduce_sum x4, other arithmetic, attend(): block_sum = jnp.sum(weight, axis=-1)  7.15 us
    convert_element_type x2, local copies, waits for them, and re-layouts, body(): local_out = jnp.transpose(result, (2, 0, 1, 3)).reshape(rows, heads_here...  6.85 us
  transfers between devices with their start and end apart: 3, of which 3 were waited for; matrix products, arithmetic and copies ran while one was open for 17% of the time, Pallas kernels for 0%

commit v1 on v0

v1 whole, which is shorter than its diff:
```python
import functools
import math

import jax
import jax.numpy as jnp
from jax import lax
from jax.experimental import pallas as pl
from jax.experimental.pallas import tpu as pltpu
from jax.sharding import PartitionSpec as P

STEPS = 4
MESH = pl.DeviceIdType.MESH
LOW = -1e30
TILES = 4


def kernel(
    cycle,
    table_ref,
    q_hbm,
    kv_hbm,
    out_ref,
    q_in,
    kv_in,
    wide,
    qg,
    kvbuf,
    result,
    outbuf,
    load_sem,
    near_send,
    far_send,
    pass_send,
    kv_recv,
    out_send,
    out_recv,
    keep_sem,
):
    me = lax.axis_index("ctx")
    side = lax.axis_index("kvh")
    core = lax.rem(me, 2)
    rows, heads, hd = q_in.shape
    kvs = kvbuf.shape[0]
    group = heads // kvs
    span = rows // 2
    tile_q = span // TILES
    tile_rows = tile_q * group
    width = group * hd
    factor = math.log2(math.e) / math.sqrt(hd)

    def ahead(n):
        return lax.rem(me + n + cycle, cycle)

    partner = me + 1 - 2 * core
    other = 1 - side

    load_kv = pltpu.make_async_copy(kv_hbm, kv_in, load_sem.at[0])
    load_kv.start()
    load_q = pltpu.make_async_copy(q_hbm, q_in, load_sem.at[1])
    load_q.start()

    barrier = pltpu.get_barrier_semaphore()
    pl.semaphore_signal(barrier, inc=1, device_id=(ahead(-2), side), device_id_type=MESH)
    pl.semaphore_signal(barrier, inc=1, device_id=(partner, side), device_id_type=MESH)
    pl.semaphore_signal(barrier, inc=1, device_id=(me, other), device_id_type=MESH)

    @pl.when(core == 0)
    def _():
        pl.semaphore_signal(barrier, inc=1, device_id=(ahead(-3), side), device_id_type=MESH)

    load_kv.wait()
    for part in range(2):
        wide[part] = kv_in[part].astype(jnp.float32)
    for g in range(kvs):
        for part in range(2):
            for s in range(2):
                kvbuf[g, part, s, 0] = wide[
                    part, pl.ds(s * span * kvs + g, span, stride=kvs), :
                ].astype(jnp.bfloat16)

    pl.semaphore_wait(barrier, 3 + core)

    far_slot = 1 + 2 * core
    pass_slot = 3 - 2 * core
    far_device = ahead(1 + 2 * core)

    def send_near(g):
        return pltpu.make_async_remote_copy(
            src_ref=kvbuf.at[g, :, :, 0],
            dst_ref=kvbuf.at[g, :, :, 2],
            send_sem=near_send.at[g],
            recv_sem=kv_recv.at[g, 2],
            device_id=(ahead(2), side),
            device_id_type=MESH,
        )

    def send_far(g):
        return pltpu.make_async_remote_copy(
            src_ref=kvbuf.at[g, :, :, 0],
            dst_ref=kvbuf.at[g, :, :, far_slot],
            send_sem=far_send.at[g],
            recv_sem=kv_recv.at[g, far_slot],
            device_id=(far_device, side),
            device_id_type=MESH,
        )

    def send_pass(g):
        return pltpu.make_async_remote_copy(
            src_ref=kvbuf.at[g, :, :, 2],
            dst_ref=kvbuf.at[g, :, :, pass_slot],
            send_sem=pass_send.at[g],
            recv_sem=kv_recv.at[g, pass_slot],
            device_id=(partner, side),
            device_id_type=MESH,
        )

    def arrival(g, slot):
        return pltpu.make_async_remote_copy(
            src_ref=kvbuf.at[g, :, :, 0],
            dst_ref=kvbuf.at[g, :, :, slot],
            send_sem=near_send.at[g],
            recv_sem=kv_recv.at[g, slot],
            device_id=(partner, side),
            device_id_type=MESH,
        )

    def columns(owner, g):
        return pl.ds(pl.multiple_of((owner * kvs + g) * width, width), width)

    def send_out(g):
        return pltpu.make_async_remote_copy(
            src_ref=outbuf.at[0, g],
            dst_ref=out_ref.at[:, columns(side, g)],
            send_sem=out_send.at[g],
            recv_sem=out_recv.at[g],
            device_id=(me, other),
            device_id_type=MESH,
        )

    def take_out(g):
        return pltpu.make_async_remote_copy(
            src_ref=outbuf.at[0, g],
            dst_ref=out_ref.at[:, columns(other, g)],
            send_sem=out_send.at[g],
            recv_sem=out_recv.at[g],
            device_id=(me, other),
            device_id_type=MESH,
        )

    def keep_out(g):
        return pltpu.make_async_copy(
            outbuf.at[1, g], out_ref.at[:, columns(side, g)], keep_sem.at[g]
        )

    for g in range(kvs):
        send_near(g).start()
        send_far(g).start()

    load_q.wait()
    for t in range(2 * TILES):
        block = q_in[t * tile_q : (t + 1) * tile_q].astype(jnp.float32)
        for g in range(kvs):
            qg[g, t * tile_rows : (t + 1) * tile_rows, :] = (
                block[:, g * group : (g + 1) * group, :]
                .reshape(tile_rows, hd)
                .astype(jnp.bfloat16)
            )

    biases = []
    for s in range(2):
        mine = table_ref[2 * me + s]
        biases.append(
            [None]
            + [
                jnp.where(table_ref[2 * ahead(-b) + s] < mine, 0.0, LOW).astype(jnp.float32)
                for b in range(1, STEPS)
            ]
        )

    def attend(g, late, slot):
        spans = 2 if late else 1
        keys = spans * STEPS * span

        def one(t, carry):
            start = pl.multiple_of(t * tile_rows, tile_rows)
            q = qg[g, pl.ds((span * group if late else 0) + start, tile_rows), :]
            k = kvbuf[g, 0, :spans].reshape(keys, hd)
            v = kvbuf[g, 1, :spans].reshape(keys, hd)
            scores = lax.dot_general(
                q, k, (((1,), (1,)), ((), ())), preferred_element_type=jnp.float32
            )
            parts = []
            for s in range(spans):
                for b in range(STEPS):
                    part = scores[:, (s * STEPS + b) * span : (s * STEPS + b + 1) * span]
                    if s == spans - 1:
                        if b == 0:
                            row = lax.broadcasted_iota(jnp.int32, part.shape, 0) // group
                            col = lax.broadcasted_iota(jnp.int32, part.shape, 1)
                            part = jnp.where(col <= row + t * tile_q, part, LOW)
                        else:
                            part = part + biases[s][b]
                    parts.append(part)
            top = functools.reduce(jnp.maximum, parts)
            top = jnp.max(top, axis=-1, keepdims=True)
            weights = jnp.concatenate(
                [jnp.exp2((part - top) * factor).astype(jnp.bfloat16) for part in parts], axis=1
            )
            both = jnp.dot(
                weights,
                jnp.concatenate([v, jnp.ones_like(v)], axis=1),
                preferred_element_type=jnp.float32,
            )
            result[pl.ds(start, tile_rows), :] = both[:, :hd] / both[:, hd:]
            first = pl.multiple_of(t * tile_q, tile_q)
            for h in range(group):
                outbuf[slot, g, pl.ds(first, tile_q), h * hd : (h + 1) * hd] = result[
                    pl.ds(start + h, tile_q, stride=group), :
                ].astype(jnp.bfloat16)
            return carry

        lax.fori_loop(0, TILES, one, 0)

    def compute(g, slot):
        late = jnp.where(slot == 0, other, side)

        @pl.when(late == 1)
        def _():
            attend(g, True, slot)

        @pl.when(late == 0)
        def _():
            attend(g, False, slot)

    arrival(0, 2).wait_recv()
    send_pass(0).start()

    def step(i, carry):
        g = i // 2
        slot = lax.rem(i, 2)

        @pl.when(slot == 0)
        def _():
            arrival(g, 1).wait_recv()
            arrival(g, 3).wait_recv()

        @pl.when(jnp.logical_and(slot == 1, g < kvs - 1))
        def _():
            arrival(g + 1, 2).wait_recv()
            send_pass(g + 1).start()

        compute(g, slot)

        @pl.when(slot == 0)
        def _():
            send_out(g).start()

        @pl.when(slot == 1)
        def _():
            keep_out(g).start()

        return carry

    lax.fori_loop(0, 2 * kvs, step, 0)

    for g in range(kvs):
        keep_out(g).wait()
        send_near(g).wait_send()
        send_far(g).wait_send()
        send_pass(g).wait_send()
    for g in range(kvs):
        send_out(g).wait_send()
        take_out(g).wait_recv()


def body(queries, key_value, span_table):
    rows, heads, hd = queries.shape
    kvs = key_value.shape[2]
    group = heads // kvs
    span = rows // 2
    cycle = lax.axis_size("ctx")
    sides = lax.axis_size("kvh")
    flat = key_value.reshape(2, rows * kvs, hd)
    dma = pltpu.SemaphoreType.DMA
    flops = 3 * 2 * 2 * span * heads * STEPS * span * hd
    return pl.pallas_call(
        functools.partial(kernel, cycle),
        out_shape=jax.ShapeDtypeStruct((rows // sides, sides * heads * hd), jnp.bfloat16),
        in_specs=[
            pl.BlockSpec(memory_space=pltpu.SMEM),
            pl.BlockSpec(memory_space=pl.ANY),
            pl.BlockSpec(memory_space=pl.ANY),
        ],
        out_specs=pl.BlockSpec(memory_space=pl.ANY),
        scratch_shapes=[
            pltpu.VMEM((rows, heads, hd), jnp.bfloat16),
            pltpu.VMEM((2, rows * kvs, hd), jnp.bfloat16),
            pltpu.VMEM((2, rows * kvs, hd), jnp.float32),
            pltpu.VMEM((kvs, rows * group, hd), jnp.bfloat16),
            pltpu.VMEM((kvs, 2, 2, STEPS, span, hd), jnp.bfloat16),
            pltpu.VMEM((span * group, hd), jnp.float32),
            pltpu.VMEM((2, kvs, span, group * hd), jnp.bfloat16),
            dma((2,)),
            dma((kvs,)),
            dma((kvs,)),
            dma((kvs,)),
            dma((kvs, STEPS)),
            dma((kvs,)),
            dma((kvs,)),
            dma((kvs,)),
        ],
        compiler_params=pltpu.CompilerParams(
            collective_id=0, has_side_effects=True, vmem_limit_bytes=40 * 1024 * 1024
        ),
        cost_estimate=pl.CostEstimate(
            flops=flops, bytes_accessed=5 * 1024 * 1024, transcendentals=flops // (4 * hd)
        ),
    )(span_table, queries, flat)


def solution(mesh):
    in_specs = (P("ctx", "kvh", None), P(None, "ctx", "kvh", None), P())
    out_specs = P(("ctx", "kvh"), None)
    return jax.shard_map(body, mesh=mesh, in_specs=in_specs, out_specs=out_specs, check_vma=False)
```

time: 95.9 us -> 45.2 us (0.47)
  Pallas kernels: 0 us -> 40.2 us
  matrix products: 27.8 us -> 0 us
  blocking collectives: 22.4 us -> 0 us
  waiting for transfers between devices: 18.7 us -> 0 us
  local copies, waits for them, and re-layouts: 17 us -> 4.61 us
  other arithmetic: 7.65 us -> 0 us
  starting transfers between devices: 1.02 us -> 0 us
    pallas_call x0 -> x1, Pallas kernels: none -> 40.2 us  [body(): pl.pallas_call(functools.partial(kernel, cycle), out_shape=jax.ShapeDtype...]
    dot_general x8 -> x0, matrix products: 27.8 us -> none  [the longest x4 19.3 us: attend(): jnp.einsum('ghqk,kgd->ghqd', weight.astype(jnp.bfloat16), block[1], prefe...]
    all_to_all x1 -> x0, blocking collectives: 22.4 us -> none  [body(): lax.all_to_all(local_out, 'kvh', split_axis=0, concat_axis=1, tiled=True)]
    ppermute x3 -> x0, waiting for transfers between devices: 18.7 us -> none  [passed_along(): return lax.ppermute(value, axis, pairs)]
    all_to_all x2 -> x0, local copies, waits for them, and re-layouts: 8.14 us -> none  [body(): lax.all_to_all(local_out, 'kvh', split_axis=0, concat_axis=1, tiled=True)]
    reduce_sum x4 -> x0, other arithmetic: 7.15 us -> none  [attend(): block_sum = jnp.sum(weight, axis=-1)]
    convert_element_type x2 -> x0, local copies, waits for them, and re-layouts: 6.85 us -> none  [body(): local_out = jnp.transpose(result, (2, 0, 1, 3)).reshape(rows, heads_here...]
    unnamed x3 -> x7, local copies, waits for them, and re-layouts: 1.26 us -> 4.61 us
  transfers between devices with their start and end apart: 3 -> 0, of which waited for: 3 -> 0; matrix products, arithmetic and copies ran while one was open for 17% -> 0% of each run, Pallas kernels for 0% -> 0%
where the time goes in v1:
time: 45.2 us; the launch traced here: 44.8 us
  Pallas kernels  40.2 us (89%)
  local copies, waits for them, and re-layouts  4.61 us (10%)
    pallas_call x1, Pallas kernels, body(): pl.pallas_call(functools.partial(kernel, cycle), out_shape=jax.ShapeDtype...  40.2 us
    unnamed x7, local copies, waits for them, and re-layouts  4.61 us

profile of v1, /device:TPU:0, one launch (start us, length us, event | category | flops | bytes accessed | tf_op | source)
XLA Modules:
  0.0 44.8 jit_solution(1988866157492533257)
XLA Ops:
  0.0 0.0 copy-start
  0.0 1.6 %copy-done = bf16[256,32,128]{2,1,0:T(8,128)(2,1)S(1)} copy-done((bf16[256,32,128]{2,1,0:T(8,128)(2,1)S(1)}, bf16[256,32,128]{2,1,0:T(8,128)(2,1)}, u32[]{:S(2)}) %copy-start) | copy-done | bytes 2097176
  1.6 0.0 copy-start.1
  1.6 1.0 %copy-done.1 = bf16[2,256,4,128]{3,2,1,0:T(4,128)(2,1)S(1)} copy-done((bf16[2,256,4,128]{3,2,1,0:T(4,128)(2,1)S(1)}, bf16[2,256,4,128]{3,2,1,0:T(4,128)(2,1)}, u32[]{:S(2)}) %copy-start.1) | copy-done | bytes 524312
  2.6 0.0 copy-start.2
  2.6 0.7 %copy-done.2 = s32[32]{0:T(128)S(1)} copy-done((s32[32]{0:T(128)S(1)}, s32[32]{0:T(128)}, u32[]{:S(2)}) %copy-start.2) | copy-done | bytes 152
  3.3 40.2 %shard_map.37 = bf16[128,8192]{1,0:T(8,128)(2,1)S(1)} custom-call(s32[32]{0:T(128)S(1)} %copy-done.2, bf16[256,32,128]{2,1,0:T(8,128)(2,1)S(1)} %copy-done, bf16[2,1024,128]{2,1,0:T(8,128)(2,1)S(1)} %bitcast.1), custom_call_target="tpu_custom_call" | custom-call | flops 3221225472 | bytes 5242880 | tf_op jit(solution)/shard_map/pallas_call | solution.py:286
  43.5 1.3 %copy.5 = bf16[128,8192]{1,0:T(8,128)(2,1)} copy(bf16[128,8192]{1,0:T(8,128)(2,1)S(1)} %shard_map.37) | data formatting | bytes 4194304
Async XLA Ops:
  0.0 1.6 %copy-start = (bf16[256,32,128]{2,1,0:T(8,128)(2,1)S(1)}, bf16[256,32,128]{2,1,0:T(8,128)(2,1)}, u32[]{:S(2)}) copy-start(bf16[256,32,128]{2,1,0:T(8,128)(2,1)} %q_hbm.1) | copy-start | bytes 6291460
  1.6 1.0 %copy-start.1 = (bf16[2,256,4,128]{3,2,1,0:T(4,128)(2,1)S(1)}, bf16[2,256,4,128]{3,2,1,0:T(4,128)(2,1)}, u32[]{:S(2)}) copy-start(bf16[2,256,4,128]{3,2,1,0:T(4,128)(2,1)} %param.4) | copy-start | bytes 1572868
  2.6 0.7 %copy-start.2 = (s32[32]{0:T(128)S(1)}, s32[32]{0:T(128)}, u32[]{:S(2)}) copy-start(s32[32]{0:T(128)} %table_ref.1) | copy-start | bytes 388

commit v2 on v1

--- a/solution.py
+++ b/solution.py
@@ -16,10 +16,11 @@
 
 def kernel(
     cycle,
-    table_ref,
+    table_hbm,
     q_hbm,
     kv_hbm,
     out_ref,
+    table_ref,
     q_in,
     kv_in,
     wide,
@@ -58,6 +59,8 @@
     load_kv.start()
     load_q = pltpu.make_async_copy(q_hbm, q_in, load_sem.at[1])
     load_q.start()
+    load_table = pltpu.make_async_copy(table_hbm, table_ref, load_sem.at[2])
+    load_table.start()
 
     barrier = pltpu.get_barrier_semaphore()
     pl.semaphore_signal(barrier, inc=1, device_id=(ahead(-2), side), device_id_type=MESH)
@@ -166,6 +169,7 @@
                 .astype(jnp.bfloat16)
             )
 
+    load_table.wait()
     biases = []
     for s in range(2):
         mine = table_ref[2 * me + s]
@@ -219,7 +223,7 @@
                 ].astype(jnp.bfloat16)
             return carry
 
-        lax.fori_loop(0, TILES, one, 0)
+        lax.fori_loop(0, TILES, one, 0, unroll=True)
 
     def compute(g, slot):
         late = jnp.where(slot == 0, other, side)
@@ -287,12 +291,13 @@
         functools.partial(kernel, cycle),
         out_shape=jax.ShapeDtypeStruct((rows // sides, sides * heads * hd), jnp.bfloat16),
         in_specs=[
-            pl.BlockSpec(memory_space=pltpu.SMEM),
+            pl.BlockSpec(memory_space=pl.ANY),
             pl.BlockSpec(memory_space=pl.ANY),
             pl.BlockSpec(memory_space=pl.ANY),
         ],
         out_specs=pl.BlockSpec(memory_space=pl.ANY),
         scratch_shapes=[
+            pltpu.SMEM(span_table.shape, jnp.int32),
             pltpu.VMEM((rows, heads, hd), jnp.bfloat16),
             pltpu.VMEM((2, rows * kvs, hd), jnp.bfloat16),
             pltpu.VMEM((2, rows * kvs, hd), jnp.float32),
@@ -300,7 +305,7 @@
             pltpu.VMEM((kvs, 2, 2, STEPS, span, hd), jnp.bfloat16),
             pltpu.VMEM((span * group, hd), jnp.float32),
             pltpu.VMEM((2, kvs, span, group * hd), jnp.bfloat16),
-            dma((2,)),
+            dma((3,)),
             dma((kvs,)),
             dma((kvs,)),
             dma((kvs,)),
@@ -310,7 +315,7 @@
             dma((kvs,)),
         ],
         compiler_params=pltpu.CompilerParams(
-            collective_id=0, has_side_effects=True, vmem_limit_bytes=40 * 1024 * 1024
+            collective_id=0, has_side_effects=True, vmem_limit_bytes=60 * 1024 * 1024
         ),
         cost_estimate=pl.CostEstimate(
             flops=flops, bytes_accessed=5 * 1024 * 1024, transcendentals=flops // (4 * hd)

time: 45.2 us -> 41.2 us (0.912)
  Pallas kernels: 40.2 us -> 37.9 us
  local copies, waits for them, and re-layouts: 4.61 us -> 3.1 us
    pallas_call x1, Pallas kernels: 40.2 us -> 37.9 us  [body(): pl.pallas_call(functools.partial(kernel, cycle), out_shape=jax.ShapeDtype...]
    unnamed x7 -> x1, local copies, waits for them, and re-layouts: 4.61 us -> 3.1 us
where the time goes in v2:
time: 41.2 us; the launch traced here: 41 us
  Pallas kernels  37.9 us (92%)
  local copies, waits for them, and re-layouts  3.1 us (8%)
    pallas_call x1, Pallas kernels, body(): pl.pallas_call(functools.partial(kernel, cycle), out_shape=jax.ShapeDtype...  37.9 us
    unnamed x1, local copies, waits for them, and re-layouts  3.1 us

profile of v2, /device:TPU:0, one launch (start us, length us, event | category | flops | bytes accessed | tf_op | source)
XLA Modules:
  0.0 41.0 jit_solution(2992172403536243502)
XLA Ops:
  0.0 37.9 %shard_map.37 = bf16[128,8192]{1,0:T(8,128)(2,1)} custom-call(s32[32]{0:T(128)} %table_hbm.1, bf16[256,32,128]{2,1,0:T(8,128)(2,1)} %q_hbm.1, bf16[2,1024,128]{2,1,0:T(8,128)(2,1)} %bitcast.1), custom_call_target="tpu_custom_call" | custom-call | flops 3221225472 | bytes 5242880 | tf_op jit(solution)/shard_map/pallas_call | solution.py:290
  37.9 3.1 %copy.5 = bf16[128,8192]{1,0:T(8,128)(2,1)} copy(bf16[128,8192]{1,0:T(8,128)(2,1)} %shard_map.37) | data formatting | bytes 4194304

commit v3 on v2

--- a/solution.py
+++ b/solution.py
@@ -36,12 +36,13 @@
     out_send,
     out_recv,
     keep_sem,
+    swap_sem,
 ):
     me = lax.axis_index("ctx")
     side = lax.axis_index("kvh")
     core = lax.rem(me, 2)
     rows, heads, hd = q_in.shape
-    kvs = kvbuf.shape[0]
+    kvs = kvbuf.shape[0] - 1
     group = heads // kvs
     span = rows // 2
     tile_q = span // TILES
@@ -127,6 +128,25 @@
             device_id_type=MESH,
         )
 
+    moved = kvs - 1
+    moved_rows = pl.ds(pl.multiple_of(other * (span * group), span * group), span * group)
+    swap_kv = pltpu.make_async_remote_copy(
+        src_ref=kvbuf.at[moved, :, :, 0],
+        dst_ref=kvbuf.at[kvs, :, :, 0],
+        send_sem=swap_sem.at[0],
+        recv_sem=swap_sem.at[1],
+        device_id=(me, other),
+        device_id_type=MESH,
+    )
+    swap_q = pltpu.make_async_remote_copy(
+        src_ref=qg.at[moved, moved_rows],
+        dst_ref=qg.at[kvs, moved_rows],
+        send_sem=swap_sem.at[2],
+        recv_sem=swap_sem.at[3],
+        device_id=(me, other),
+        device_id_type=MESH,
+    )
+
     def columns(owner, g):
         return pl.ds(pl.multiple_of((owner * kvs + g) * width, width), width)
 
@@ -152,22 +172,33 @@
 
     def keep_out(g):
         return pltpu.make_async_copy(
-            outbuf.at[1, g], out_ref.at[:, columns(side, g)], keep_sem.at[g]
-        )
-
+            outbuf.at[1, g],
+            out_ref.at[:, columns(jnp.where(g == kvs, other, side), jnp.minimum(g, moved))],
+            keep_sem.at[g],
+        )
+
+    swap_kv.start()
     for g in range(kvs):
         send_near(g).start()
         send_far(g).start()
 
     load_q.wait()
-    for t in range(2 * TILES):
-        block = q_in[t * tile_q : (t + 1) * tile_q].astype(jnp.float32)
-        for g in range(kvs):
-            qg[g, t * tile_rows : (t + 1) * tile_rows, :] = (
+    def regroup(g, s):
+        for t in range(TILES):
+            first = pl.multiple_of(s * span + t * tile_q, tile_q)
+            block = q_in[pl.ds(first, tile_q)].astype(jnp.float32)
+            qg[g, pl.ds(pl.multiple_of(first * group, tile_rows), tile_rows), :] = (
                 block[:, g * group : (g + 1) * group, :]
                 .reshape(tile_rows, hd)
                 .astype(jnp.bfloat16)
             )
+
+    regroup(moved, other)
+    swap_q.start()
+    regroup(moved, side)
+    for g in range(kvs - 1):
+        regroup(g, 0)
+        regroup(g, 1)
 
     load_table.wait()
     biases = []
@@ -236,23 +267,31 @@
         def _():
             attend(g, False, slot)
 
+    swap_kv.wait_recv()
+    send_near(kvs).start()
+    send_far(kvs).start()
     arrival(0, 2).wait_recv()
     send_pass(0).start()
+    pairs = 2 * (kvs - 1)
 
     def step(i, carry):
-        g = i // 2
-        slot = lax.rem(i, 2)
-
-        @pl.when(slot == 0)
+        g = jnp.where(i < pairs, i // 2, i - moved)
+        slot = jnp.where(i < pairs, lax.rem(i, 2), 1)
+
+        @pl.when(jnp.logical_or(slot == 0, i >= pairs))
         def _():
             arrival(g, 1).wait_recv()
             arrival(g, 3).wait_recv()
 
-        @pl.when(jnp.logical_and(slot == 1, g < kvs - 1))
+        @pl.when(jnp.logical_and(slot == 1, g < kvs))
         def _():
             arrival(g + 1, 2).wait_recv()
             send_pass(g + 1).start()
 
+        @pl.when(g == kvs)
+        def _():
+            swap_q.wait_recv()
+
         compute(g, slot)
 
         @pl.when(slot == 0)
@@ -267,12 +306,14 @@
 
     lax.fori_loop(0, 2 * kvs, step, 0)
 
-    for g in range(kvs):
+    swap_kv.wait_send()
+    swap_q.wait_send()
+    for g in range(kvs + 1):
         keep_out(g).wait()
         send_near(g).wait_send()
         send_far(g).wait_send()
         send_pass(g).wait_send()
-    for g in range(kvs):
+    for g in range(moved):
         send_out(g).wait_send()
         take_out(g).wait_recv()
 
@@ -301,18 +342,19 @@
             pltpu.VMEM((rows, heads, hd), jnp.bfloat16),
             pltpu.VMEM((2, rows * kvs, hd), jnp.bfloat16),
             pltpu.VMEM((2, rows * kvs, hd), jnp.float32),
-            pltpu.VMEM((kvs, rows * group, hd), jnp.bfloat16),
-            pltpu.VMEM((kvs, 2, 2, STEPS, span, hd), jnp.bfloat16),
+            pltpu.VMEM((kvs + 1, rows * group, hd), jnp.bfloat16),
+            pltpu.VMEM((kvs + 1, 2, 2, STEPS, span, hd), jnp.bfloat16),
             pltpu.VMEM((span * group, hd), jnp.float32),
-            pltpu.VMEM((2, kvs, span, group * hd), jnp.bfloat16),
+            pltpu.VMEM((2, kvs + 1, span, group * hd), jnp.bfloat16),
             dma((3,)),
+            dma((kvs + 1,)),
+            dma((kvs + 1,)),
+            dma((kvs + 1,)),
+            dma((kvs + 1, STEPS)),
             dma((kvs,)),
             dma((kvs,)),
-            dma((kvs,)),
-            dma((kvs, STEPS)),
-            dma((kvs,)),
-            dma((kvs,)),
-            dma((kvs,)),
+            dma((kvs + 1,)),
+            dma((4,)),
         ],
         compiler_params=pltpu.CompilerParams(
             collective_id=0, has_side_effects=True, vmem_limit_bytes=60 * 1024 * 1024

time: 41.2 us -> 35.7 us (0.87)
  Pallas kernels: 37.9 us -> 32.4 us
    pallas_call x1, Pallas kernels: 37.9 us -> 32.4 us  [body(): pl.pallas_call(functools.partial(kernel, cycle), out_shape=jax.ShapeDtype...]
where the time goes in v3:
time: 35.7 us; the launch traced here: 35.5 us
  Pallas kernels  32.4 us (91%)
  local copies, waits for them, and re-layouts  3.1 us (9%)
    pallas_call x1, Pallas kernels, body(): pl.pallas_call(functools.partial(kernel, cycle), out_shape=jax.ShapeDtype...  32.4 us
    unnamed x1, local copies, waits for them, and re-layouts  3.1 us

profile of v3, /device:TPU:0, one launch (start us, length us, event | category | flops | bytes accessed | tf_op | source)
XLA Modules:
  0.0 35.5 jit_solution(11568604770043108644)
XLA Ops:
  0.0 32.4 %shard_map.37 = bf16[128,8192]{1,0:T(8,128)(2,1)} custom-call(s32[32]{0:T(128)} %table_hbm.1, bf16[256,32,128]{2,1,0:T(8,128)(2,1)} %q_hbm.1, bf16[2,1024,128]{2,1,0:T(8,128)(2,1)} %bitcast.1), custom_call_target="tpu_custom_call" | custom-call | flops 3221225472 | bytes 5242880 | tf_op jit(solution)/shard_map/pallas_call | solution.py:331
  32.4 3.1 %copy.5 = bf16[128,8192]{1,0:T(8,128)(2,1)} copy(bf16[128,8192]{1,0:T(8,128)(2,1)} %shard_map.37) | data formatting | bytes 4194304

commit v4 on v3

--- a/solution.py
+++ b/solution.py
@@ -75,13 +75,16 @@
     load_kv.wait()
     for part in range(2):
         wide[part] = kv_in[part].astype(jnp.float32)
-    for g in range(kvs):
+
+    def split(g):
         for part in range(2):
             for s in range(2):
                 kvbuf[g, part, s, 0] = wide[
                     part, pl.ds(s * span * kvs + g, span, stride=kvs), :
                 ].astype(jnp.bfloat16)
 
+    split(kvs - 1)
+    split(0)
     pl.semaphore_wait(barrier, 3 + core)
 
     far_slot = 1 + 2 * core
@@ -178,10 +181,8 @@
         )
 
     swap_kv.start()
-    for g in range(kvs):
-        send_near(g).start()
-        send_far(g).start()
-
+    send_near(0).start()
+    send_far(0).start()
     load_q.wait()
     def regroup(g, s):
         for t in range(TILES):
@@ -195,6 +196,11 @@
 
     regroup(moved, other)
     swap_q.start()
+    for g in range(1, kvs):
+        if g < moved:
+            split(g)
+        send_near(g).start()
+        send_far(g).start()
     regroup(moved, side)
     for g in range(kvs - 1):
         regroup(g, 0)
@@ -357,7 +363,7 @@
             dma((4,)),
         ],
         compiler_params=pltpu.CompilerParams(
-            collective_id=0, has_side_effects=True, vmem_limit_bytes=60 * 1024 * 1024
+            collective_id=0, has_side_effects=True, vmem_limit_bytes=int(51 * 1024 * 1024)
         ),
         cost_estimate=pl.CostEstimate(
             flops=flops, bytes_accessed=5 * 1024 * 1024, transcendentals=flops // (4 * hd)

time: 35.7 us -> 35.2 us (0.986)
  Pallas kernels: 32.4 us -> 32 us
    pallas_call x1, Pallas kernels: 32.4 us -> 32 us  [body(): pl.pallas_call(functools.partial(kernel, cycle), out_shape=jax.ShapeDtype...]
    unnamed x1 -> x5, local copies, waits for them, and re-layouts: 3.1 us -> 3.02 us
where the time goes in v4:
time: 35.2 us; the launch traced here: 35 us
  Pallas kernels  32 us (91%)
  local copies, waits for them, and re-layouts  3.02 us (9%)
    pallas_call x1, Pallas kernels, body(): pl.pallas_call(functools.partial(kernel, cycle), out_shape=jax.ShapeDtype...  32 us
    unnamed x5, local copies, waits for them, and re-layouts  3.02 us

profile of v4, /device:TPU:0, one launch (start us, length us, event | category | flops | bytes accessed | tf_op | source)
XLA Modules:
  0.0 35.0 jit_solution(17702306982325283107)
XLA Ops:
  0.0 0.0 copy-start
  0.0 1.0 %copy-done = bf16[2,256,4,128]{3,2,1,0:T(4,128)(2,1)S(1)} copy-done((bf16[2,256,4,128]{3,2,1,0:T(4,128)(2,1)S(1)}, bf16[2,256,4,128]{3,2,1,0:T(4,128)(2,1)}, u32[]{:S(2)}) %copy-start) | copy-done | bytes 524312
  1.0 0.0 copy-start.1
  1.0 0.7 %copy-done.1 = s32[32]{0:T(128)S(1)} copy-done((s32[32]{0:T(128)S(1)}, s32[32]{0:T(128)}, u32[]{:S(2)}) %copy-start.1) | copy-done | bytes 152
  1.7 32.0 %shard_map.37 = bf16[128,8192]{1,0:T(8,128)(2,1)S(1)} custom-call(s32[32]{0:T(128)S(1)} %copy-done.1, bf16[256,32,128]{2,1,0:T(8,128)(2,1)} %q_hbm.1, bf16[2,1024,128]{2,1,0:T(8,128)(2,1)S(1)} %bitcast.1), custom_call_target="tpu_custom_call" | custom-call | flops 3221225472 | bytes 5242880 | tf_op jit(solution)/shard_map/pallas_call | solution.py:337
  33.7 1.3 %copy.5 = bf16[128,8192]{1,0:T(8,128)(2,1)} copy(bf16[128,8192]{1,0:T(8,128)(2,1)S(1)} %shard_map.37) | data formatting | bytes 4194304
Async XLA Ops:
  0.0 1.0 %copy-start = (bf16[2,256,4,128]{3,2,1,0:T(4,128)(2,1)S(1)}, bf16[2,256,4,128]{3,2,1,0:T(4,128)(2,1)}, u32[]{:S(2)}) copy-start(bf16[2,256,4,128]{3,2,1,0:T(4,128)(2,1)} %param.4) | copy-start | bytes 1572868
  1.0 0.7 %copy-start.1 = (s32[32]{0:T(128)S(1)}, s32[32]{0:T(128)}, u32[]{:S(2)}) copy-start(s32[32]{0:T(128)} %table_hbm.1) | copy-start | bytes 388
